TPU v7x, 32 devices: a whole 2x2x4 slice. The times are simulated.
32 devices in a mesh: groups: 2 (over y), row: 8 (over z, x), col: 2 (over core).
Axes of the slice: x: 2, y: 2, z: 4, core: 2. Of those that a mesh axis runs over, the one named last changes fastest.
Arguments:
- coeffs: float32 [16384, 128], P(('groups', 'row')), parts along dimension 0, may hold values from -0.4 to 0.4
- blocks: float32 [4096, 4096], P(('groups', 'row')), parts along dimension 0, may hold values from -0.75 to 0.75
- block_list: int32 [4096, 2], P(('groups', 'row')), parts along dimension 0, may hold values from 0 to 127
- block_count: int32 [16], P(('groups', 'row')), parts along dimension 0, may hold values from 32 to 256, as said below
Outputs:
- exchange_out: float32 [16384, 128], P(('groups', 'row', 'col')), parts along dimension 0
There are 2 independent parts, one for each index of `groups`. A program takes and returns all parts, laid end to end along the dimension named above; each array names one. Nothing has to cross between parts.
Inputs may be any that keep to these rules, and one draw needn't show every extreme that they name: Only the first block_count[p] slots of fitting function p are screened in; some fitting function fills all 256 slots.
All inputs are finite; a program needn't handle non-finite values.
Results may differ from a plain program's by a relative error of at most 0.0003.
Values sent between devices are 32-bit elements; how exact they have to be, the bound alone decides.
A program may use at most 64 MiB of HBM per device.

v0:
```python
import jax
import jax.numpy as jnp
from jax import lax
from jax.sharding import PartitionSpec as P

BLK = 64


def body(coeffs, blocks, block_list, block_count):
    full_coeffs = lax.all_gather(coeffs, "row", axis=0, tiled=True)
    total_rows, occupied = full_coeffs.shape
    half_width = occupied // lax.axis_size("col")
    halves = lax.dynamic_slice_in_dim(
        full_coeffs, lax.axis_index("col") * half_width, half_width, 1
    )
    block_edge = BLK
    segments = total_rows // block_edge
    coeff_table = halves.reshape(segments, block_edge, half_width)
    slot_total = blocks.shape[0]
    group_size = slot_total // 4
    live_count = block_count[0]
    group_count = (live_count + group_size - 1) // group_size

    def accumulate(round_index, slab_table):
        first_slot = round_index * group_size
        chosen = lax.dynamic_slice_in_dim(block_list, first_slot, group_size, 0)
        pieces = lax.dynamic_slice_in_dim(blocks, first_slot, group_size, 0).reshape(
            group_size, block_edge, block_edge
        )
        picked = coeff_table[chosen[:, 1]]
        product = jnp.einsum(
            "sml,slj->smj",
            pieces,
            picked,
            precision=lax.Precision.HIGHEST,
            preferred_element_type=jnp.float32,
        )
        in_use = first_slot + jnp.arange(group_size) < live_count
        row_select = (
            (chosen[:, 0][None, :] == jnp.arange(segments)[:, None]) & in_use[None, :]
        ).astype(jnp.float32)
        flat_product = product.reshape(group_size, block_edge * half_width)
        return slab_table + jnp.dot(
            row_select,
            flat_product,
            precision=lax.Precision.HIGHEST,
            preferred_element_type=jnp.float32,
        )

    slab_table = lax.fori_loop(
        0, group_count, accumulate, jnp.zeros((segments, block_edge * half_width), jnp.float32)
    )
    slab = slab_table.reshape(total_rows, half_width)
    projected = jnp.dot(
        slab.T, full_coeffs, precision=lax.Precision.HIGHEST, preferred_element_type=jnp.float32
    )
    arrived_slabs = lax.all_to_all(slab[None], "row", split_axis=1, concat_axis=0, tiled=True)
    partial_value = jnp.einsum(
        "pmj,pji->mi",
        arrived_slabs,
        lax.all_gather(projected[None], "row", axis=0, tiled=True),
        precision=lax.Precision.HIGHEST,
        preferred_element_type=jnp.float32,
    )
    return lax.psum_scatter(partial_value, "col", scatter_dimension=0, tiled=True)


def solution(mesh):
    in_specs = (
        P(("groups", "row"), None),
        P(("groups", "row"), None),
        P(("groups", "row"), None),
        P(("groups", "row")),
    )
    out_specs = P(("groups", "row", "col"), None)
    return jax.shard_map(body, mesh=mesh, in_specs=in_specs, out_specs=out_specs, check_vma=False)
```

profile of v0, /device:TPU:0, one launch (start us, length us, event | category | flops | bytes accessed | tf_op | source)
XLA Modules:
  0.0 320.4 jit_solution(5378320068981468309)
XLA Ops:
  7.9 77.7 %all-gather.3.cloned.1.call-done = f32[8192,128]{1,0:T(8,128)} async-done(((f32[1024,128]{1,0:T(8,128)}), f32[8192,128]{1,0:T(8,128)}) %all-gather.3.cloned.1.call-update) | async-done | bytes 4194320 | tf_op jit(solution)/shard_map/all_gather | solution.py:10
  85.6 5.3 %constant_dynamic-slice_fusion.2 = f32[8192,64]{1,0:T(8,128)} fusion(f32[8192,128]{1,0:T(8,128)} %all-gather.3.cloned.1.call-done, s32[]{:T(128)S(6)} %select_n.17), kind=kLoop, calls=%fused_computation.15 | loop fusion | bytes 4194308 | tf_op jit(solution)/shard_map/dynamic_slice | solution.py:13
  90.9 1.6 broadcast_in_dim.7
  92.5 34.6 %while.10 = (s32[]{:T(128)}, f32[128,4096]{1,0:T(8,128)}, s32[]{:T(128)}, s32[256,2]{0,1:T(2,128)S(1)}, s32[]{:T(128)}, /*index=5*/f32[256,4096]{1,0:T(8,128)}, ...) while((s32[]{:T(128)}, f32[128,4096]{1,0:T(8,128)}, s32[]{:T(128)}, ...), condition=%wide.region_1.2_spmd, body=%wide.region_0.1_spmd.sunk | while | flops 604521792 | bytes 33561696 | solution.py:50
  92.6 2.9 gather_fusion
  96.8 2.2 reshape.41
  99.0 5.1 %fusion.23 = f32[64,64,64]{2,1,0:T(8,128)} fusion(f32[64,64,64]{2,1,0:T(8,128)} %reshape.41, f32[64,64,64]{2,1,0:T(8,128)S(1)} %gather_fusion), kind=kOutput, calls=%fused_computation.16.clone.1 | convolution fusion | flops 201326592 | bytes 3145728 | tf_op jit(solution)/shard_map/while/body/sml,slj->smj/dot_general | solution.py:31
  104.1 2.3 reshape.42
  109.9 2.9 gather_fusion
  114.1 2.2 reshape.41
  116.3 5.1 %fusion.23 = f32[64,64,64]{2,1,0:T(8,128)} fusion(f32[64,64,64]{2,1,0:T(8,128)} %reshape.41, f32[64,64,64]{2,1,0:T(8,128)S(1)} %gather_fusion), kind=kOutput, calls=%fused_computation.16.clone.1 | convolution fusion | flops 201326592 | bytes 3145728 | tf_op jit(solution)/shard_map/while/body/sml,slj->smj/dot_general | solution.py:31
  121.4 2.3 reshape.42
  127.1 4.6 %broadcast_in_dim_reshape.3 = f32[1,8192,64]{2,1,0:T(8,128)} reshape(f32[128,4096]{1,0:T(8,128)} %get-tuple-element.43) | data formatting | bytes 4194304 | tf_op jit(solution)/shard_map/broadcast_in_dim;reshape | solution.py:57
  132.2 38.4 %reduce = f32[8192,64]{1,0:T(8,128)} reduce(f32[8192,1,64]{2,1,0:T(1,128)} %bitcast.30, f32[]{:T(128)} %broadcast.23), dimensions={1}, to_apply=%bitcast.11.reduce_sub_computation | reduce | bytes 4194308
  170.7 7.2 %reshape.33 = f32[8,1,65536]{2,1,0:T(1,128)} reshape(f32[8192,64]{1,0:T(8,128)} %reduce) | data formatting | bytes 4194304
  177.9 36.9 %all-to-all-start = ((f32[8,1,65536]{2,1,0:T(1,128)}), f32[8,1,65536]{2,1,0:T(1,128)}, u32[]{:S(2)}, u32[]{:S(2)}) async-start(f32[8,1,65536]{2,1,0:T(1,128)} %reshape.33), calls=%async_computation | async-start | bytes 4194304 | tf_op jit(solution)/shard_map/all_to_all | solution.py:57
  215.0 3.1 reshape.22
  218.1 10.4 %fusion.7 = f32[64,128]{1,0:T(8,128)S(1)} fusion(f32[8192,64]{1,0:T(8,128)} %reshape.22, f32[8192,128]{1,0:T(8,128)} %all-gather.3.cloned.1.call-done), kind=kOutput, calls=%fused_computation.17 | convolution fusion | flops 805306368 | bytes 6324224 | tf_op jit(solution)/shard_map/dot_general | solution.py:54
  228.5 54.0 %all-gather = f32[512,128]{1,0:T(8,128)S(1)} all-gather(f32[64,128]{1,0:T(8,128)S(1)} %fusion.7), channel_id=2, replica_groups=mesh['groups'=2,'row'=8,'col'=2] {'row'}, dimensions={0}, use_global_device_ids=true | all-gather | bytes 294912 | tf_op jit(solution)/shard_map/all_gather | solution.py:61
  282.5 7.2 %reduce.1 = f32[8,65536]{1,0:T(8,128)S(1)} reduce(f32[8,1,65536]{2,1,0:T(1,128)} %all-to-all-done, f32[]{:T(128)} %broadcast.23), dimensions={1}, to_apply=%all_to_all.4.reduce_sub_computation | reduce | bytes 4194308 | tf_op jit(solution)/shard_map/all_to_all | solution.py:57
  289.8 7.1 %reshape.34 = f32[8192,1,64]{2,1,0:T(1,128)} reshape(f32[8,65536]{1,0:T(8,128)S(1)} %reduce.1) | data formatting | bytes 4194304
  296.9 3.4 %copy.10 = f32[8,1024,64]{1,0,2:T(8,128)S(1)} copy(f32[8,1024,64]{2,1,0:T(8,128)} %bitcast.29) | data formatting | bytes 4194304 | tf_op jit(solution)/shard_map/all_to_all | solution.py:57
  300.3 4.2 %convolution_bitcast_fusion = f32[1024,128]{1,0:T(8,128)} fusion(f32[8,1024,64]{1,0,2:T(8,128)S(1)} %copy.10, f32[8,64,128]{2,1,0:T(8,128)S(1)} %bitcast.31), kind=kOutput, calls=%fused_computation.13 | convolution fusion | flops 805306368 | bytes 2883584 | tf_op jit(solution)/shard_map/pmj,pji->mi/dot_general | solution.py:58
  304.6 9.0 %reduce-scatter.2.cloned.1.call-done = f32[512,128]{1,0:T(8,128)} async-done(((f32[1024,128]{1,0:T(8,128)}), f32[512,128]{1,0:T(8,128)}) %reduce-scatter.2.cloned.1.call-update) | async-done | bytes 262160 | tf_op jit(solution)/shard_map/reduce_scatter | solution.py:65
  (30 shorter events, 11.1 us)
Async XLA Ops:
  6.5 79.1 %all-gather.3.cloned.1.call-start = ((), (), s32[]{:S(2)}) async-start(), calls=%async_computation.2 | async-start | bytes 4718592 | tf_op jit(solution)/shard_map/all_gather | solution.py:10
  90.9 1.6 copy-start.3
  104.1 2.9 copy-start
  108.5 1.3 copy-start.1
  121.4 2.9 copy-start
  125.8 1.3 copy-start.1
  177.9 37.1 %copy-start.2 = (f32[128,4096]{1,0:T(8,128)S(1)}, f32[128,4096]{1,0:T(8,128)}, u32[]{:S(2)}) copy-start(f32[128,4096]{1,0:T(8,128)} %get-tuple-element.43) | copy-start | bytes 6291460
  177.9 104.7 %all-to-all-start = ((f32[8,1,65536]{2,1,0:T(1,128)}), f32[8,1,65536]{2,1,0:T(1,128)}, u32[]{:S(2)}, u32[]{:S(2)}) async-start(f32[8,1,65536]{2,1,0:T(1,128)} %reshape.33), calls=%async_computation | async-start | bytes 4194304 | tf_op jit(solution)/shard_map/all_to_all | solution.py:57
  214.7 98.8 %reduce-scatter.2.cloned.1.call-start = ((), (), s32[]{:S(2)}) async-start(), calls=%async_computation.3 | async-start | bytes 786432 | tf_op jit(solution)/shard_map/reduce_scatter | solution.py:65
Sparse Core Ops, SparseCore 0:
  9.5 76.0 all-gather.2
  304.7 8.8 reduce-scatter.1
where the time goes:
time: 320 us
  waiting for transfers between devices  87.4 us (27%)
  blocking collectives  54 us (17%)
  local copies, waits for them, and re-layouts  52.9 us (17%)
  other arithmetic  47 us (15%)
  starting transfers between devices  37.1 us (12%)
  matrix products  27.7 us (9%)
  between operations  14.1 us (4%)
    all_gather x1, waiting for transfers between devices, body(): full_coeffs = lax.all_gather(coeffs, 'row', axis=0, tiled=True)  77.7 us
    all_gather x1, blocking collectives, body(): lax.all_gather(projected[None], 'row', axis=0, tiled=True)  54 us
    unnamed x1, other arithmetic  38.4 us
    all_to_all x1, starting transfers between devices, body(): lax.all_to_all(slab[None], 'row', split_axis=1, concat_axis=0, tiled=True)  36.9 us
    unnamed x7, local copies, waits for them, and re-layouts  14.9 us
    dot_general x1, matrix products, body(): jnp.dot(slab.T, full_coeffs, precision=lax.Precision.HIGHEST, preferred_e...  10.4 us
    dot_general x2, matrix products, accumulate(): jnp.einsum('sml,slj->smj', pieces, picked, precision=lax.Precision.HIGHES...  10.2 us
    reduce_scatter x1, waiting for transfers between devices, body(): lax.psum_scatter(partial_value, 'col', scatter_dimension=0, tiled=True)  9 us
  transfers between devices with their start and end apart: 3, of which 2 were waited for; matrix products, arithmetic and copies ran while one was open for 4% of the time, Pallas kernels for 0%

commit v1 on v0

--- a/solution.py
+++ b/solution.py
@@ -1,12 +1,401 @@
 import jax
 import jax.numpy as jnp
 from jax import lax
+from jax.experimental import pallas as pl
+from jax.experimental.pallas import tpu as pltpu
 from jax.sharding import PartitionSpec as P
 
 BLK = 64
-
-
-def body(coeffs, blocks, block_list, block_count):
+LINE = 4
+F32 = jnp.float32
+BF16 = jnp.bfloat16
+
+
+def split(value):
+    high = value.astype(BF16)
+    low = (value - high.astype(F32)).astype(BF16)
+    return high, low
+
+
+def mul(a, b):
+    return jnp.dot(a, b, preferred_element_type=F32)
+
+
+def mul_t(a, b):
+    return lax.dot_general(a, b, (((0,), (0,)), ((), ())), preferred_element_type=F32)
+
+
+def kernel(
+    columns, rows, count, coeffs, blocks, out,
+    full, tiles, pieces, table, prod, slab, proj, pbd, pbl,
+    own, sib_out, sib_in, x_in, up_in, dn_in,
+    blk_sem, ag_line, ag_x, ag_sib, rs_sib, rs_x, rs_line,
+):
+    row = lax.axis_index("row")
+    z, x, c = lax.div(row, 2), lax.rem(row, 2), lax.axis_index("col")
+    shard = coeffs.shape[0]
+    half = shard // 2
+    segs = full.shape[0] // BLK
+    slots = blocks.shape[0]
+    lanes = 128
+    kk = blocks.shape[1] // lanes
+    chunk = half // 2
+    has_dn, has_up = z > 0, z < LINE - 1
+
+    def send(src, dst, send_sem, recv_sem, where):
+        return pltpu.make_async_remote_copy(
+            src_ref=src, dst_ref=dst, send_sem=send_sem, recv_sem=recv_sem,
+            device_id=where, device_id_type=pl.DeviceIdType.MESH,
+        )
+
+    up, down, across, mate = {"row": row + 2}, {"row": row - 2}, {"row": row + 1 - 2 * x}, {"col": 1 - c}
+
+    def fetch(k):
+        return pltpu.make_async_copy(
+            blocks.at[:, pl.ds(k * lanes, lanes)], tiles.at[pl.ds(k * slots, slots), :], blk_sem.at[k]
+        )
+
+    for k in range(kk):
+        fetch(k).start()
+
+    barrier = pltpu.get_barrier_semaphore()
+
+    def greet(where):
+        pl.semaphore_signal(barrier, inc=1, device_id=where, device_id_type=pl.DeviceIdType.MESH)
+
+    greet(across)
+    greet(mate)
+    pl.when(has_up)(lambda: greet(up))
+    pl.when(has_dn)(lambda: greet(down))
+    pl.semaphore_wait(barrier, 2 + lax.div(z + LINE - 2, LINE - 1) + lax.div(2 * LINE - 3 - z, LINE - 1))
+
+    def piece(zz, xx, cc):
+        start = (zz * 2 + xx) * shard + cc * half
+        return full.at[pl.ds(pl.multiple_of(start, half), half), :]
+
+    def line_copy(way, step, zz, src=None):
+        here = piece(zz, x, c)
+        return send(here if src is None else src, here, ag_line.at[0, way, step], ag_line.at[1, way, step],
+                    up if way == 0 else down)
+
+    def x_copy(zz, src=None, xx=None):
+        here = piece(zz, x if xx is None else xx, c)
+        return send(here if src is None else src, here, ag_x.at[0, zz], ag_x.at[1, zz], across)
+
+    def sib_copy(zz, xx, cc):
+        here = piece(zz, xx, cc)
+        return send(here, here, ag_sib.at[0, zz * 2 + xx], ag_sib.at[1, zz * 2 + xx], mate)
+
+    mine = coeffs.at[pl.ds(pl.multiple_of(c * half, half), half), :]
+    pl.when(has_up)(lambda: line_copy(0, 0, z, mine).start())
+    pl.when(has_dn)(lambda: line_copy(1, 0, z, mine).start())
+    x_copy(z, mine).start()
+
+    full[pl.ds(pl.multiple_of(row * shard, shard), shard), :] = coeffs[...]
+
+    left = lax.broadcasted_iota(jnp.int32, (BLK, lanes), 1) < BLK
+
+    def build(zz, xx, cc):
+        first = (zz * 2 + xx) * (shard // BLK) + cc * (half // BLK)
+
+        def one(q, carry):
+            seg = first + q
+            value = full[pl.ds(pl.multiple_of(seg * BLK, BLK), BLK), :]
+            turned = pltpu.roll(value, BLK, 1)
+            flag = jnp.broadcast_to(c, (BLK, lanes)) == 0
+            top = jnp.where(left, jnp.where(flag, value, turned), 0.0)
+            bottom = jnp.where(left, 0.0, jnp.where(flag, turned, value))
+            table[seg, :BLK, :lanes], table[seg, :BLK, lanes:] = split(top)
+            table[seg, BLK:, :lanes], table[seg, BLK:, lanes:] = split(bottom)
+            return carry
+
+        lax.fori_loop(0, half // BLK, one, 0, unroll=UNROLL_TABLE)
+
+    def prepare(first, last):
+        def one(s, carry):
+            high, low = split(tiles[pl.ds(s, kk, stride=slots), :])
+            pieces[s, :kk, :] = high
+            pieces[s, kk:, :] = low
+            return carry
+
+        lax.fori_loop(first, last, one, 0, unroll=UNROLL_PREP)
+
+    for k in range(kk):
+        fetch(k).wait()
+    prepare(0, slots // 2)
+    build(z, x, 0)
+    build(z, x, 1)
+
+    def arrived(way, step):
+        zz = z - step if way == 0 else z + step
+
+        @pl.when(z >= step if way == 0 else z + step < LINE)
+        def _():
+            line_copy(way, step - 1, zz).wait_recv()
+            if step < LINE - 1:
+                pl.when(has_up if way == 0 else has_dn)(lambda: line_copy(way, step, zz).start())
+            x_copy(zz).start()
+            sib_copy(zz, x, c).start()
+        return zz
+
+    def exists(way, step, act):
+        zz = z - step if way == 0 else z + step
+        pl.when(z >= step if way == 0 else z + step < LINE)(lambda: act(zz))
+
+    def crossed(zz):
+        x_copy(zz, xx=1 - x).wait_recv()
+        sib_copy(zz, 1 - x, c).start()
+
+    def build_line(zz):
+        build(zz, x, c)
+
+    def build_far(zz):
+        build(zz, 1 - x, c)
+
+    def build_mate(zz):
+        sib_copy(zz, x, 1 - c).wait_recv()
+        build(zz, x, 1 - c)
+
+    def build_mate_far(zz):
+        sib_copy(zz, 1 - x, 1 - c).wait_recv()
+        build(zz, 1 - x, 1 - c)
+
+    for step in range(1, LINE + 1):
+        if step < LINE:
+            for way in (0, 1):
+                arrived(way, step)
+        if step == 1:
+            crossed(z)
+            prepare(slots // 2, slots)
+            build_far(z)
+        else:
+            for way in (0, 1):
+                exists(way, step - 1, crossed)
+            for way in (0, 1):
+                exists(way, step - 1, build_far)
+        if step < LINE:
+            for way in (0, 1):
+                exists(way, step, build_line)
+            for way in (0, 1):
+                exists(way, step, build_mate)
+        if step == 2:
+            build_mate_far(z)
+        if step > 2:
+            for way in (0, 1):
+                exists(way, step - 2, build_mate_far)
+    for way in (0, 1):
+        exists(way, LINE - 1, build_mate_far)
+
+    def slot(s, carry):
+        value = mul(pieces[s], table[columns[s]])
+        low = value[kk:, :lanes] + value[kk:, lanes:]
+        prod[pl.ds(s, kk, stride=slots), :] = value[:kk, :lanes] + (value[:kk, lanes:] + low)
+        return carry
+
+    lax.fori_loop(0, slots, slot, 0, unroll=UNROLL_SLOT)
+
+    at_seg = lax.broadcasted_iota(jnp.int32, (segs, slots), 0) == rows[...]
+    in_use = lax.broadcasted_iota(jnp.int32, (segs, slots), 1) < count[...]
+    select = jnp.where(at_seg & in_use, 1.0, 0.0).astype(BF16)
+    proj[...] = jnp.zeros_like(proj)
+
+    def assemble(k, carry):
+        high, low = split(prod[pl.ds(pl.multiple_of(k * slots, slots), slots), :])
+        both = mul(select, jnp.concatenate([high, low], axis=1))
+        part = both[:, :lanes] + both[:, lanes:]
+        slab[pl.ds(k, segs, stride=kk), :] = part
+        part_high, part_low = split(part)
+        pair = jnp.concatenate(
+            [full[pl.ds(2 * k, segs, stride=BLK), :], full[pl.ds(2 * k + 1, segs, stride=BLK), :]], axis=1
+        )
+        pair_high, pair_low = split(pair)
+        proj[...] += mul_t(
+            jnp.concatenate([part_high, part_low], axis=0), jnp.concatenate([pair_high, pair_high], axis=0)
+        ) + mul_t(part_high, pair_low)
+        return carry
+
+    lax.fori_loop(0, kk, assemble, 0, unroll=UNROLL_ASM)
+
+    projected = proj[:BLK, :lanes] + proj[BLK:, lanes:]
+    high, low = split(projected)
+    blank = jnp.zeros((BLK, lanes), BF16)
+    for base in (0, 2 * BLK):
+        pbd[base:base + BLK, :lanes] = high
+        pbd[base:base + BLK, lanes:] = blank
+        pbd[base + BLK:base + 2 * BLK, :lanes] = blank
+        pbd[base + BLK:base + 2 * BLK, lanes:] = high
+    pbl[:BLK, :lanes] = low
+    pbl[:BLK, lanes:] = blank
+    pbl[BLK:, :lanes] = blank
+    pbl[BLK:, lanes:] = low
+
+    def value_of(zz, xx, cc):
+        start = (zz * 2 + xx) * 2 * chunk + cc * chunk
+        high, low = split(slab[pl.ds(pl.multiple_of(start, chunk), chunk), :])
+        return mul(jnp.concatenate([high, low], axis=1), pbd[...]) + mul(high, pbl[...])
+
+    side, mirror = lax.div(z, 2), z + lax.div(z, 2) * (LINE - 1 - 2 * z)
+
+    def flip(value):
+        return value + side * (LINE - 1 - 2 * value)
+
+    order = [flip(jnp.int32(3)), flip(jnp.int32(2)), flip(1 - mirror), flip(mirror)]
+
+    def mate_copy(d, e):
+        at = d * 2 + e
+        return send(sib_out.at[at], sib_in.at[at], rs_sib.at[0, at], rs_sib.at[1, at], mate)
+
+    def cross_copy(d):
+        return send(own.at[d * 2 + 1 - x], x_in.at[d], rs_x.at[0, d], rs_x.at[1, d], across)
+
+    def up_copy(d):
+        return send(own.at[d * 2 + x], up_in.at[d], rs_line.at[0, 0, d], rs_line.at[1, 0, d], up)
+
+    def dn_copy(d):
+        return send(own.at[d * 2 + x], dn_in.at[d], rs_line.at[0, 1, d], rs_line.at[1, 1, d], down)
+
+    def to_mate(d, e):
+        sib_out[d * 2 + e] = value_of(d, e, 1 - c)
+        mate_copy(d, e).start()
+
+    def keep(d, e):
+        own[d * 2 + e] = value_of(d, e, c)
+
+    def add_mate(d, e):
+        mate_copy(d, e).wait_recv()
+        own[d * 2 + e] += sib_in[d * 2 + e]
+
+    to_mate(order[0], 1 - x)
+    for i in range(LINE):
+        d = order[i]
+        keep(d, 1 - x)
+        if i + 1 < LINE:
+            to_mate(order[i + 1], 1 - x)
+        else:
+            to_mate(order[0], x)
+        add_mate(d, 1 - x)
+        cross_copy(d).start()
+    for i in range(LINE):
+        d = order[i]
+        keep(d, x)
+        if i + 1 < LINE:
+            to_mate(order[i + 1], x)
+        add_mate(d, x)
+    for i in range(LINE - 1):
+        d = order[i]
+        cross_copy(d).wait_recv()
+        own[d * 2 + x] += x_in[d]
+
+        @pl.when(d > z)
+        def _():
+            @pl.when(has_dn)
+            def _():
+                up_copy(d).wait_recv()
+                own[d * 2 + x] += up_in[d]
+            up_copy(d).start()
+
+        @pl.when(d < z)
+        def _():
+            @pl.when(has_up)
+            def _():
+                dn_copy(d).wait_recv()
+                own[d * 2 + x] += dn_in[d]
+            dn_copy(d).start()
+
+    cross_copy(z).wait_recv()
+    own[z * 2 + x] += x_in[z]
+
+    @pl.when(has_dn)
+    def _():
+        up_copy(z).wait_recv()
+        own[z * 2 + x] += up_in[z]
+
+    @pl.when(has_up)
+    def _():
+        dn_copy(z).wait_recv()
+        own[z * 2 + x] += dn_in[z]
+
+    out[pl.ds(0, chunk, stride=2), :] = own[z * 2 + x, :, :lanes]
+    out[pl.ds(1, chunk, stride=2), :] = own[z * 2 + x, :, lanes:]
+
+    for way in (0, 1):
+        edge = has_up if way == 0 else has_dn
+        pl.when(edge)(lambda way=way: line_copy(way, 0, z, mine).wait_send())
+        for step in range(1, LINE):
+            def done(zz, way=way, step=step, edge=edge):
+                if step < LINE - 1:
+                    pl.when(edge)(lambda: line_copy(way, step, zz).wait_send())
+                x_copy(zz).wait_send()
+                sib_copy(zz, x, c).wait_send()
+                sib_copy(zz, 1 - x, c).wait_send()
+            exists(way, step, done)
+    x_copy(z, mine).wait_send()
+    sib_copy(z, 1 - x, c).wait_send()
+    for d in range(LINE):
+        for e in (0, 1):
+            mate_copy(d, e).wait_send()
+        cross_copy(d).wait_send()
+        pl.when(d > z)(lambda d=d: up_copy(d).wait_send())
+        pl.when(d < z)(lambda d=d: dn_copy(d).wait_send())
+
+
+UNROLL_TABLE = 2
+UNROLL_PREP = 8
+UNROLL_SLOT = 8
+UNROLL_ASM = 2
+
+
+def exchange(coeffs, blocks, block_list, block_count):
+    shard, occupied = coeffs.shape
+    slots, flat = blocks.shape
+    total = shard * lax.axis_size("row")
+    half = shard // 2
+    chunk = half // 2
+    lanes = 128
+    kk = flat // lanes
+    segs = total // BLK
+    listed = block_list.T
+    wide = 2 * lanes
+    vmem = pl.BlockSpec(memory_space=pltpu.VMEM)
+    dma = pltpu.SemaphoreType.DMA
+    return pl.pallas_call(
+        kernel,
+        out_shape=jax.ShapeDtypeStruct((half, occupied), F32),
+        in_specs=[
+            pl.BlockSpec(memory_space=pltpu.SMEM), vmem, vmem, vmem, pl.BlockSpec(memory_space=pl.ANY),
+        ],
+        out_specs=vmem,
+        scratch_shapes=[
+            pltpu.VMEM((total, occupied), F32),
+            pltpu.VMEM((slots * kk, lanes), F32),
+            pltpu.VMEM((slots, 2 * kk, lanes), BF16),
+            pltpu.VMEM((segs, 2 * BLK, wide), BF16),
+            pltpu.VMEM((slots * kk, lanes), F32),
+            pltpu.VMEM((segs * kk, lanes), F32),
+            pltpu.VMEM((lanes, wide), F32),
+            pltpu.VMEM((2 * lanes, wide), BF16),
+            pltpu.VMEM((lanes, wide), BF16),
+            pltpu.VMEM((2 * LINE, chunk, wide), F32),
+            pltpu.VMEM((2 * LINE, chunk, wide), F32),
+            pltpu.VMEM((2 * LINE, chunk, wide), F32),
+            pltpu.VMEM((LINE, chunk, wide), F32),
+            pltpu.VMEM((LINE, chunk, wide), F32),
+            pltpu.VMEM((LINE, chunk, wide), F32),
+            dma((kk,)),
+            dma((2, 2, LINE - 1)),
+            dma((2, LINE)),
+            dma((2, 2 * LINE)),
+            dma((2, 2 * LINE)),
+            dma((2, LINE)),
+            dma((2, 2, LINE)),
+        ],
+        compiler_params=pltpu.CompilerParams(
+            collective_id=0, has_side_effects=True, vmem_limit_bytes=56 * 1024 * 1024
+        ),
+    )(listed[1], listed[:1], block_count[:, None], coeffs, blocks)
+
+
+def plain(coeffs, blocks, block_list, block_count):
     full_coeffs = lax.all_gather(coeffs, "row", axis=0, tiled=True)
     total_rows, occupied = full_coeffs.shape
     half_width = occupied // lax.axis_size("col")
@@ -65,6 +454,12 @@
     return lax.psum_scatter(partial_value, "col", scatter_dimension=0, tiled=True)
 
 
+def body(coeffs, blocks, block_list, block_count):
+    if lax.axis_size("row") == 2 * LINE and lax.axis_size("col") == 2:
+        return exchange(coeffs, blocks, block_list, block_count)
+    return plain(coeffs, blocks, block_list, block_count)
+
+
 def solution(mesh):
     in_specs = (
         P(("groups", "row"), None),

time: 320 us -> 82.7 us (0.26)
  waiting for transfers between devices: 87.4 us -> 0 us
  Pallas kernels: 0 us -> 78.8 us
  blocking collectives: 54 us -> 0 us
  local copies, waits for them, and re-layouts: 52.9 us -> 3.01 us
  other arithmetic: 47 us -> 0 us
  starting transfers between devices: 37.1 us -> 0 us
  matrix products: 27.7 us -> 0 us
  between operations: 14.1 us -> 0.66 us
    pallas_call x0 -> x1, Pallas kernels: none -> 78.8 us  [exchange(): pl.pallas_call(kernel, out_shape=jax.ShapeDtypeStruct((half, occupied), F...]
    all_gather x1 -> x0, waiting for transfers between devices: 77.7 us -> none  [body(): full_coeffs = lax.all_gather(coeffs, 'row', axis=0, tiled=True)]
    all_gather x1 -> x0, blocking collectives: 54 us -> none  [body(): lax.all_gather(projected[None], 'row', axis=0, tiled=True)]
    unnamed x1 -> x0, other arithmetic: 38.4 us -> none
    all_to_all x1 -> x0, starting transfers between devices: 36.9 us -> none  [body(): lax.all_to_all(slab[None], 'row', split_axis=1, concat_axis=0, tiled=True)]
    dot_general x6 -> x0, matrix products: 27.7 us -> none  [the longest x1 10.4 us: body(): jnp.dot(slab.T, full_coeffs, precision=lax.Precision.HIGHEST, preferred_e...]
    unnamed x7 -> x1, local copies, waits for them, and re-layouts: 14.9 us -> 1.67 us
    reshape x5 -> x0, local copies, waits for them, and re-layouts: 12 us -> none  [the longest x2 4.55 us: accumulate(): flat_product = product.reshape(group_size, block_edge * half_width)]
  transfers between devices with their start and end apart: 3 -> 0, of which waited for: 2 -> 0; matrix products, arithmetic and copies ran while one was open for 4% -> 0% of each run, Pallas kernels for 0% -> 0%
where the time goes in v1:
time: 82.7 us; the launch traced here: 82.5 us
  Pallas kernels  78.8 us (95%)
  local copies, waits for them, and re-layouts  3.01 us (4%)
    pallas_call x1, Pallas kernels, exchange(): pl.pallas_call(kernel, out_shape=jax.ShapeDtypeStruct((half, occupied), F...  78.8 us
    unnamed x1, local copies, waits for them, and re-layouts  1.67 us

profile of v1, /device:TPU:0, one launch (start us, length us, event | category | flops | bytes accessed | tf_op | source)
XLA Modules:
  0.0 82.5 jit_solution(6873880087001358510)
XLA Ops:
  0.7 1.3 %fusion = (s32[1,256]{1,0:T(1,128)}, s32[1,256]{1,0:T(1,128)}) fusion(s32[2,256]{1,0:T(2,128)} %bitcast.5), kind=kLoop, calls=%fused_computation | loop fusion | bytes 4096 | tf_op jit(solution)/shard_map/slice | solution.py:395
  2.0 78.8 %shard_map.46 = f32[512,128]{1,0:T(8,128)} custom-call(s32[256]{0:T(256)} %bitcast.4, s32[1,256]{1,0:T(1,128)} %get-tuple-element.5.rows, s32[1,1]{1,0:T(1,128)} %bitcast.3.count, f32[1024,128]{1,0:T(8,128)} %coeffs.1, f32[256,4096]{1,0:T(8,128)} %blocks.1), custom_call_target="tpu_custom_call" | custom-call | tf_op jit(solution)/shard_map/pallas_call | solution.py:361
  80.8 1.7 %copy.7 = f32[512,128]{1,0:T(8,128)} copy(f32[512,128]{1,0:T(8,128)} %shard_map.46) | data formatting | bytes 524288
